TPU v7x, 256 devices: a whole 4x4x8 slice. The times are simulated.
256 devices in a mesh: pb: 16 (over y, x), kv: 16 (over z, core).
Axes of the slice: x: 4, y: 4, z: 8, core: 2. Of those that a mesh axis runs over, the one named last changes fastest.
Arguments:
- query: bfloat16 [4096, 128, 192], P('pb', 'kv'), may hold values from -12 to 12
- w_uk: bfloat16 [128, 128, 512], P('kv'), may hold values from -0.5 to 0.5
- w_uv: bfloat16 [128, 512, 128], P('kv'), may hold values from -1 to 1
- kv_cache: bfloat16 [32768, 576], P('kv'), may hold values from -6 to 6
- stretch_latent: bfloat16 [4096, 576], P('pb'), may hold values from -6 to 6
- selection: int32 [64, 30], P('pb'), may hold values from 0 to 511, as said below
Outputs:
- attended: bfloat16 [4096, 16384], P('pb', 'kv')
Inputs may be any that keep to these rules, and one draw needn't show every extreme that they name: `selection`: each row lists 30 distinct cached blocks in increasing order; of one row at most 3 lie among the blocks j * 32 to (j + 1) * 32 - 1 of any j, and in every row some j holds exactly 3.
All inputs are finite; a program needn't handle non-finite values.
Results may differ from a plain program's by a relative error of at most 0.009.
Values may be sent and summed in bfloat16 or wider, within the bound.
A program may use at most 128 MiB of HBM per device.

v0:
```python
import math

import jax
import jax.numpy as jnp
from jax import lax
from jax.sharding import PartitionSpec as P

NOPE = 128
LATENT = 512
BLOCK = 64
WIN = 2


NEG = -1e30


def shifted(value, axis, steps):
    count = lax.axis_size(axis)
    initial, last = (max(0, -steps), min(count, count - steps))
    return lax.ppermute(value, axis, [(source, source + steps) for source in range(initial, last)])


def online_update(carry, query_rows, key_rows, valid, softmax_scale):
    top, total, acc = carry
    logit_scores = (
        jnp.einsum("sqz,smz->sqm", query_rows, key_rows, preferred_element_type=jnp.float32)
        * softmax_scale
    )
    logit_scores = jnp.where(valid, logit_scores, NEG)
    fresh = jnp.maximum(top, jnp.max(logit_scores, axis=2))
    weights = jnp.where(valid, jnp.exp(logit_scores - fresh[:, :, None]), 0.0)
    factor = jnp.exp(top - fresh)
    total = total * factor + jnp.sum(weights, axis=2)
    latents = key_rows[:, :, :LATENT]
    acc = acc * factor[:, :, None] + jnp.einsum(
        "brk,bkl->brl", weights.astype(jnp.bfloat16), latents, preferred_element_type=jnp.float32
    )
    return (fresh, total, acc)


def holder_counts(selection, kb_dev, holders_total):
    owner = selection // kb_dev
    holders = jnp.arange(holders_total, dtype=jnp.int32)
    return jnp.sum((owner[:, :, None] == holders[None, None, :]).astype(jnp.int32), axis=1)


def pack_tiles(kv_cache, selection, holder, slot_total):
    width = kv_cache.shape[1]
    kb_dev = kv_cache.shape[0] // BLOCK
    blocks_count = selection.shape[0]
    local = selection - holder * kb_dev
    owned = (local >= 0) & (local < kb_dev)
    rank = jnp.cumsum(owned.astype(jnp.int32), axis=1) - 1
    slots = jnp.arange(slot_total, dtype=jnp.int32)
    match = owned[:, None, :] & (rank[:, None, :] == slots[None, :, None])
    index = jnp.sum(jnp.where(match, local[:, None, :], 0), axis=2)
    filled = jnp.any(match, axis=2)
    tiles = kv_cache.reshape(kb_dev, BLOCK, width)[index]
    tiles = jnp.where(filled[:, :, None, None], tiles, jnp.zeros((), tiles.dtype))
    return tiles.reshape(blocks_count * slot_total * BLOCK, width)


def window_mask(block_global, query_index):
    key_index = (block_global[:, None] - (WIN - 1)) * BLOCK + jnp.arange(
        WIN * BLOCK, dtype=jnp.int32
    )[None, :]
    return (key_index[:, None, :] >= 0) & (key_index[:, None, :] <= query_index[:, :, None])


def fold_tiles(carry, query_rows, tiles_each, counts_each, softmax_scale):
    count, count_blocks, slot_rows, width = tiles_each.shape
    key_rows = jnp.transpose(tiles_each, (1, 0, 2, 3)).reshape(
        count_blocks, count * slot_rows, width
    )
    slot_of = jnp.arange(slot_rows, dtype=jnp.int32) // BLOCK
    valid = slot_of[None, None, :] < counts_each[:, :, None]
    valid = valid.reshape(count_blocks, 1, count * slot_rows)
    return online_update(carry, query_rows, key_rows, valid, softmax_scale)


def start_state(query_rows, query_index, block_global, keys_near, softmax_scale):
    count_blocks, rows, width = query_rows.shape
    initial = (
        jnp.full((count_blocks, rows), NEG, jnp.float32),
        jnp.zeros((count_blocks, rows), jnp.float32),
        jnp.zeros((count_blocks, rows, LATENT), jnp.float32),
    )
    return online_update(
        initial, query_rows, keys_near, window_mask(block_global, query_index), softmax_scale
    )


def per_device(query, w_uk, w_uv, kv_cache, stretch_latent, selection):
    kv_heads_total = lax.axis_size("kv")
    holder = lax.axis_index("kv")
    band = lax.axis_index("pb")
    tok, hloc, qwidth = query.shape
    width = kv_cache.shape[1]
    kb_dev = kv_cache.shape[0] // BLOCK
    nblocks = tok // BLOCK
    slot_total = max(2, 2 * selection.shape[1] // kv_heads_total)
    slot_rows = slot_total * BLOCK
    softmax_scale = 1.0 / math.sqrt(qwidth)
    absorbed = jnp.einsum(
        "thn,hnl->thl", query[:, :, :NOPE], w_uk, preferred_element_type=jnp.float32
    ).astype(jnp.bfloat16)
    full = jnp.concatenate([absorbed, query[:, :, NOPE:]], axis=2)
    recent = shifted(stretch_latent[tok - (WIN - 1) * BLOCK :], "pb", 1)
    extended = jnp.concatenate([recent, stretch_latent], axis=0)
    windows = jnp.concatenate(
        [
            extended[w * BLOCK : (w + nblocks) * BLOCK].reshape(nblocks, BLOCK, width)
            for w in range(WIN)
        ],
        axis=1,
    )
    tiles = pack_tiles(kv_cache, selection, holder, slot_total)
    counts = holder_counts(selection, kb_dev, kv_heads_total)
    query_rows = full.reshape(nblocks, BLOCK * hloc, width)
    row_token = jnp.arange(BLOCK * hloc, dtype=jnp.int32) // hloc
    block_global = band * nblocks + jnp.arange(nblocks, dtype=jnp.int32)
    query_index = block_global[:, None] * BLOCK + row_token[None, :]
    state = start_state(query_rows, query_index, block_global, windows, softmax_scale)
    per_holder = nblocks * slot_rows
    piece = lax.all_gather(tiles, "kv", axis=0, tiled=True)
    count = piece.shape[0] // per_holder
    tiles_each = piece.reshape(count, nblocks, slot_rows, width)
    top, total, acc = fold_tiles(state, query_rows, tiles_each, counts, softmax_scale)
    latent_out = (acc / total[:, :, None]).astype(jnp.bfloat16).reshape(tok, hloc, LATENT)
    attended = jnp.einsum("thl,hlv->thv", latent_out, w_uv, preferred_element_type=jnp.float32)
    return attended.astype(jnp.bfloat16).reshape(tok, hloc * w_uv.shape[2])


def solution(mesh):
    placed = (
        P("pb", "kv", None),
        P("kv", None, None),
        P("kv", None, None),
        P("kv", None),
        P("pb", None),
        P("pb", None),
    )
    return jax.shard_map(
        per_device, mesh=mesh, in_specs=placed, out_specs=P("pb", "kv"), check_vma=False
    )
```

profile of v0, /device:TPU:1, one launch (start us, length us, event | category | flops | bytes accessed | tf_op | source)
XLA Modules:
  0.0 187.2 jit_solution(15145797268379105423)
XLA Ops:
  6.5 0.0 copy-start
  6.5 0.0 copy-start.8
  6.5 0.0 copy-start.7
  6.5 0.0 copy-start.6
  6.5 0.0 all-gather.2.cloned.1.call-start
  6.6 0.8 fusion.52
  7.4 0.2 reduce_window_sum.11
  7.6 0.1 fusion.38
  7.8 0.2 select_reduce_fusion
  7.9 0.1 copy.44
  8.0 0.1 copy.46
  8.1 0.1 reshape.206
  8.2 0.1 broadcast_in_dim.87
  8.3 0.1 broadcast_in_dim.88
  8.4 4.3 %copy.45 = bf16[2048,576]{1,0:T(8,128)(2,1)} copy(bf16[2048,576]{0,1:T(8,128)(2,1)} %param.9) | data formatting | bytes 4718592 | tf_op args[3]
  12.7 2.5 %gather_fusion = bf16[12,64,576]{2,1,0:T(8,128)(2,1)S(1)} fusion(bf16[32,64,576]{2,1,0:T(8,128)(2,1)} %bitcast.28, s32[1024]{0:T(1024)S(1)} %pad_clamp_fusion), kind=kCustom, calls=%fused_computation | custom fusion | bytes 1769520 | tf_op jit(solution)/shard_map/gather | solution.py:58
  15.2 1.1 bitcast_select_fusion
  16.4 0.0 all-gather.2.cloned.1.call-update
  16.4 0.0 copy-done.7
  16.4 0.2 copy.36
  16.6 0.0 copy-start.2
  16.6 4.6 %collective-permute-start = (bf16[64,576]{1,0:T(8,128)(2,1)S(1)}, bf16[64,576]{1,0:T(8,128)(2,1)}, u32[]{:S(2)}, u32[]{:S(2)}) collective-permute-start(bf16[64,576]{1,0:T(8,128)(2,1)S(1)} %slice.26), channel_id=1, source_target_pairs={{0,16},{16,32},{32,48},{48,64},{64,80},{80,96},{96,112},{112,128},... | collective-permute-start | bytes 221192 | tf_op jit(solution)/shard_map/ppermute | solution.py:20
  21.2 0.1 lt.38
  21.3 0.0 copy-done.8
  21.3 0.1 convert_reduce_fusion
  21.5 0.1 lt.40
  21.5 0.1 lt.41
  21.6 0.0 copy-done.6
  21.6 0.7 slice.19
  22.4 0.1 broadcast_compare_fusion.1
  22.5 0.1 iota_add_fusion
  22.5 0.1 broadcast_add_fusion
  22.6 0.0 copy-done
  22.6 0.8 convert_bitcast_fusion
  23.4 0.0 copy-done.2
  23.4 0.0 copy-start.3
  23.4 1.2 pad_maximum_fusion
  24.6 2.0 %copy.40 = bf16[4,64,576]{1,2,0:T(8,128)(2,1)} copy(bf16[4,64,576]{2,1,0:T(8,128)(2,1)} %bitcast.29) | data formatting | bytes 589824 | tf_op jit(solution)/shard_map/reshape | solution.py:112
  26.6 3.4 %copy.35 = bf16[256,8,576]{2,1,0:T(8,128)(2,1)} copy(bf16[256,8,576]{0,2,1:T(8,128)(2,1)S(1)} %pad_maximum_fusion) | data formatting | bytes 4718592 | tf_op jit(solution)/shard_map/concatenate | solution.py:107
  30.0 0.0 collective-permute-done
  30.0 0.0 copy-done.3
  30.0 0.9 pad_maximum_fusion.1
  30.9 0.3 copy.39
  31.2 3.6 %fusion.53 = (f32[4,512]{1,0:T(4,128)S(1)}, f32[4,512,128]{1,2,0:T(8,128)S(1)}) fusion(bf16[4,512,576]{2,1,0:T(8,128)(2,1)} %bitcast.30, bf16[4,64,576]{1,2,0:T(8,128)(2,1)} %copy.40, bf16[4,64,576]{1,2,0:T(8,128)(2,1)S(1)} %copy.39, s32[4,512]{1,0:T(4,128)S(1)} %broadcast_add_fusion, s32[4,128]{1,0:T(4,128)S(1)} %iota_add_fusion, ...), kind=kOutput, calls=%fused_computation.88 | convolution fusion | flops 304478208 | bytes 4016640 | tf_op jit(solution)/shard_map/sqz,smz->sqm/dot_general | solution.py:26
  34.9 76.4 %all-gather.2.cloned.1.call-done = bf16[12288,576]{1,0:T(8,128)(2,1)} async-done(((bf16[768,576]{1,0:T(8,128)(2,1)}), bf16[12288,576]{1,0:T(8,128)(2,1)}) %all-gather.2.cloned.1.call-update) | async-done | bytes 14155792 | tf_op jit(solution)/shard_map/all_gather | solution.py:125
  111.2 0.0 copy-start.4
  111.2 13.6 %copy.47 = bf16[4,16,192,576]{3,2,1,0:T(8,128)(2,1)} copy(bf16[4,16,192,576]{3,2,0,1:T(8,128)(2,1)} %bitcast.25) | data formatting | bytes 28311552 | tf_op jit(solution)/shard_map/transpose | solution.py:72
  124.8 0.0 copy-done.4
  124.8 0.0 copy-start.5
  124.8 18.6 %fusion = (f32[4,512]{1,0:T(4,128)S(1)}, f32[4,512,3072]{2,1,0:T(8,128)}) fusion(pred[4,3072]{1,0:T(4,128)(4,1)S(1)} %broadcast_compare_fusion, bf16[4,512,576]{2,1,0:T(8,128)(2,1)S(1)} %bitcast.31, bf16[4,3072,576]{2,1,0:T(8,128)(2,1)} %bitcast.26), kind=kOutput, calls=%fused_computation.3 | convolution fusion | flops 7266629632 | bytes 41701376 | tf_op jit(solution)/shard_map/sqz,smz->sqm/dot_general | solution.py:26
  143.4 0.4 fusion.21
  143.8 0.0 copy-done.5
  143.8 3.1 %fusion.26 = f32[4,512,512]{2,1,0:T(8,128)} fusion(f32[4,512,128]{1,2,0:T(8,128)S(1)} %get-tuple-element.14, bf16[4,64,576]{1,2,0:T(8,128)(2,1)S(1)} %copy-done.5, bf16[4,64,576]{1,2,0:T(8,128)(2,1)S(1)} %copy.39, f32[4,512]{1,0:T(4,128)S(1)} %get-tuple-element.12, s32[4,512]{1,0:T(4,128)S(1)} %broadcast_add_fusion, s32[4,128]{1,0:T(4,128)S(1)} %iota_add_fusion, ...), kind=kOutput, calls=%fused_computation.29 | convolution fusion | flops 270794752 | bytes 5851648 | tf_op jit(solution)/shard_map/brk,bkl->brl/dot_general | solution.py:35
  146.9 11.7 %fusion.1 = f32[4,512]{1,0:T(4,128)S(1)} fusion(f32[4,512,3072]{2,1,0:T(8,128)} %get-tuple-element.16, f32[4,512]{1,0:T(4,128)S(1)} %get-tuple-element.11, pred[4,3072]{1,0:T(4,128)(4,1)S(1)} %broadcast_compare_fusion), kind=kLoop, calls=%fused_computation.4 | loop fusion | flops 31455232 | bytes 25194496 | tf_op jit(solution)/shard_map/reduce_sum | solution.py:33
  158.6 0.0 copy-start.9
  158.6 0.0 copy-start.1
  158.6 18.2 %divide_convert_fusion = bf16[4,512,512]{2,1,0:T(8,128)(2,1)} fusion(f32[4,512,512]{2,1,0:T(8,128)} %fusion.26, bf16[4,3072,576]{2,1,0:T(8,128)(2,1)} %bitcast.27, f32[4,512,3072]{2,1,0:T(8,128)} %get-tuple-element.16, f32[4,512]{1,0:T(4,128)S(1)} %get-tuple-element.11, pred[4,3072]{1,0:T(4,128)(4,1)S(1)} %broadcast_compare_fusion, ...), kind=kOutput, calls=%fused_computation.13 | convolution fusion | flops 6479151104 | bytes 44085248 | tf_op jit(solution)/shard_map/brk,bkl->brl/dot_general | solution.py:35
  176.9 0.0 copy-done.9
  176.9 2.5 %fusion.18 = bf16[8,256,128]{1,2,0:T(8,128)(2,1)S(1)} fusion(bf16[8,512,128]{2,1,0:T(8,128)(2,1)S(1)} %copy-done.9, bf16[256,8,512]{2,1,0:T(8,128)(2,1)} %bitcast.34), kind=kOutput, calls=%fused_computation.20 | convolution fusion | flops 268697600 | bytes 3670016 | tf_op jit(solution)/shard_map/thl,hlv->thv/dot_general | solution.py:130
  179.3 1.0 copy.52
  180.3 0.0 copy-done.1
  (12 shorter events, 0.1 us)
Async XLA Ops:
  6.5 16.1 %copy-start = (bf16[8,128,512]{2,1,0:T(8,128)(2,1)S(1)}, bf16[8,128,512]{2,1,0:T(8,128)(2,1)}, u32[]{:S(2)}) copy-start(bf16[8,128,512]{2,1,0:T(8,128)(2,1)} %param.7) | copy-start | bytes 3145732
  6.5 14.8 %copy-start.8 = (s32[4,30]{1,0:T(4,128)S(1)}, s32[4,30]{1,0:T(4,128)}, u32[]{:S(2)}) copy-start(s32[4,30]{1,0:T(4,128)} %param.11) | copy-start | bytes 1444
  6.5 9.8 %copy-start.7 = (bf16[256,576]{0,1:T(8,128)(2,1)S(1)}, bf16[256,576]{0,1:T(8,128)(2,1)}, u32[]{:S(2)}) copy-start(bf16[256,576]{0,1:T(8,128)(2,1)} %param.10) | copy-start | bytes 884740
  6.5 15.1 %copy-start.6 = (bf16[256,8,192]{0,2,1:T(8,128)(2,1)S(1)}, bf16[256,8,192]{0,2,1:T(8,128)(2,1)}, u32[]{:S(2)}) copy-start(bf16[256,8,192]{0,2,1:T(8,128)(2,1)} %param.6) | copy-start | bytes 2359300
  6.5 104.7 %all-gather.2.cloned.1.call-start = ((), (), s32[]{:S(2)}) async-start(), calls=%async_computation | async-start | bytes 16711680 | tf_op jit(solution)/shard_map/all_gather | solution.py:125
  16.6 6.8 %copy-start.2 = (bf16[256,576]{1,0:T(8,128)(2,1)}, bf16[256,576]{1,0:T(8,128)(2,1)S(1)}, u32[]{:S(2)}) copy-start(bf16[256,576]{1,0:T(8,128)(2,1)S(1)} %copy.36) | copy-start | bytes 884740
  16.6 13.4 %collective-permute-start = (bf16[64,576]{1,0:T(8,128)(2,1)S(1)}, bf16[64,576]{1,0:T(8,128)(2,1)}, u32[]{:S(2)}, u32[]{:S(2)}) collective-permute-start(bf16[64,576]{1,0:T(8,128)(2,1)S(1)} %slice.26), channel_id=1, source_target_pairs={{0,16},{16,32},{32,48},{48,64},{64,80},{80,96},{96,112},{112,128},... | collective-permute-start | bytes 221192 | tf_op jit(solution)/shard_map/ppermute | solution.py:20
  23.4 6.6 %copy-start.3 = (bf16[256,576]{1,0:T(8,128)(2,1)S(1)}, bf16[256,576]{1,0:T(8,128)(2,1)}, u32[]{:S(2)}) copy-start(bf16[256,576]{1,0:T(8,128)(2,1)} %copy-done.2) | copy-start | bytes 884740
  111.2 13.6 %copy-start.4 = (bf16[256,8,576]{2,1,0:T(8,128)(2,1)S(1)}, bf16[256,8,576]{2,1,0:T(8,128)(2,1)}, u32[]{:S(2)}) copy-start(bf16[256,8,576]{2,1,0:T(8,128)(2,1)} %copy.35) | copy-start | bytes 7077892
  124.8 19.0 %copy-start.5 = (bf16[4,64,576]{1,2,0:T(8,128)(2,1)S(1)}, bf16[4,64,576]{1,2,0:T(8,128)(2,1)}, u32[]{:S(2)}) copy-start(bf16[4,64,576]{1,2,0:T(8,128)(2,1)} %copy.40) | copy-start | bytes 884740
  158.6 18.3 %copy-start.9 = (bf16[8,512,128]{2,1,0:T(8,128)(2,1)S(1)}, bf16[8,512,128]{2,1,0:T(8,128)(2,1)}, u32[]{:S(2)}) copy-start(bf16[8,512,128]{2,1,0:T(8,128)(2,1)} %param.8) | copy-start | bytes 3145732
  158.6 21.7 %copy-start.1 = (bf16[8,128,512]{2,1,0:T(8,128)(2,1)S(1)}, bf16[8,128,512]{2,1,0:T(8,128)(2,1)}, u32[]{:S(2)}) copy-start(bf16[8,128,512]{2,1,0:T(8,128)(2,1)} %param.7) | copy-start | bytes 3145732
Sparse Core Ops, SparseCore 0:
  16.5 94.6 all-gather.1
where the time goes:
time: 188 us; the launch traced here: 187 us
  waiting for transfers between devices  76.4 us (41%)
  matrix products  46.8 us (25%)
  local copies, waits for them, and re-layouts  28.8 us (15%)
  other arithmetic  17 us (9%)
  between operations  13.6 us (7%)
  starting transfers between devices  4.62 us (2%)
    all_gather x1, waiting for transfers between devices, per_device(): piece = lax.all_gather(tiles, 'kv', axis=0, tiled=True)  76.4 us
    dot_general x2, matrix products, online_update(): jnp.einsum('sqz,smz->sqm', query_rows, key_rows, preferred_element_type=j...  22.2 us
    dot_general x2, matrix products, online_update(): jnp.einsum('brk,bkl->brl', weights.astype(jnp.bfloat16), latents, preferr...  21.3 us
    transpose x1, local copies, waits for them, and re-layouts, fold_tiles(): jnp.transpose(tiles_each, (1, 0, 2, 3))  13.6 us
    reduce_sum x2, other arithmetic, online_update(): total = total * factor + jnp.sum(weights, axis=2)  12 us
    unnamed x22, local copies, waits for them, and re-layouts  4.59 us
    ppermute x1, starting transfers between devices, shifted(): lax.ppermute(value, axis, [(source, source + steps) for source in range(i...  4.58 us
  transfers between devices with their start and end apart: 2, of which 1 were waited for; matrix products, arithmetic and copies ran while one was open for 7% of the time, Pallas kernels for 0%

commit v1 on v0

v1 whole, which is shorter than its diff:
```python
import functools
import math

import jax
import jax.numpy as jnp
from jax import lax
from jax.experimental import pallas as pl
from jax.experimental.pallas import tpu as pltpu
from jax.sharding import PartitionSpec as P

NOPE = 128
ROPE = 64
LATENT = 512
WIDTH = LATENT + ROPE
VDIM = 128
BLOCK = 64
LANES = 128
CAP = 3
NEG = -1e30
MESH = pl.DeviceIdType.MESH
F32 = jnp.float32
BF16 = jnp.bfloat16


def transposed_dot(a, b):
    return lax.dot_general(a, b, (((0,), (0,)), ((), ())), preferred_element_type=F32)


def swap_halves(x):
    return jnp.concatenate([x[:, BLOCK:], x[:, :BLOCK]], axis=1)


def kernel(
    pb_total, kv_total, scale,
    sel_ref, query_hbm, uk_hbm, uv_hbm, kv_hbm, near_hbm,
    out_ref,
    kv_v, query_v, uk_v, uv_v, near_v, before_v, full_v, ring_v, twin_v, acc_v, top_v, total_v, latent_v, count_ref,
    load_sem, kv_sem, near_send, near_recv, ring_send, ring_recv, twin_send, twin_recv,
):
    heads = query_v.shape[0]
    tok = query_v.shape[2]
    blocks = tok // BLOCK
    pairs = blocks // 2
    chips = kv_total // 2
    kb_dev = 2 * kv_v.shape[0]
    pb = lax.axis_index("pb")
    kv = lax.axis_index("kv")
    chip = kv // 2
    core = kv % 2
    ahead = (chip + 1 - 2 * core + chips) % chips
    behind = (chip - 1 + 2 * core + chips) % chips
    to_next = (pb, 2 * ahead + core)
    to_prev = (pb, 2 * behind + core)
    to_twin = (pb, 2 * chip + 1 - core)
    to_right = ((pb + 1) % pb_total, kv)
    to_left = ((pb + pb_total - 1) % pb_total, kv)

    def load_kv(i):
        return pltpu.make_async_copy(
            kv_hbm.at[:, pl.ds(i * LANES, LANES)], kv_v.at[i], kv_sem.at[i]
        )

    load_near = pltpu.make_async_copy(near_hbm, near_v, load_sem.at[0])
    load_query = pltpu.make_async_copy(query_hbm, query_v, load_sem.at[1])
    load_uk = pltpu.make_async_copy(uk_hbm, uk_v, load_sem.at[2])
    load_uv = pltpu.make_async_copy(uv_hbm, uv_v, load_sem.at[3])
    for i in range(kv_v.shape[0]):
        load_kv(i).start()
    load_near.start()
    load_query.start()
    load_uk.start()
    load_uv.start()

    barrier = pltpu.get_barrier_semaphore()
    partners = (to_next, to_prev, to_twin, to_right, to_left)
    for partner in partners:
        pl.semaphore_signal(barrier, inc=1, device_id=partner, device_id_type=MESH)

    low = lax.broadcasted_iota(jnp.int32, (WIDTH, LANES), 1) < BLOCK

    def ring_copy(step, pair):
        slot = step * pairs + pair
        return pltpu.make_async_remote_copy(
            src_ref=ring_v.at[slot], dst_ref=ring_v.at[slot + pairs],
            send_sem=ring_send.at[slot], recv_sem=ring_recv.at[slot + pairs],
            device_id=to_next, device_id_type=MESH,
        )

    def twin_copy(slot):
        return pltpu.make_async_remote_copy(
            src_ref=ring_v.at[slot], dst_ref=twin_v.at[slot],
            send_sem=twin_send.at[slot], recv_sem=twin_recv.at[slot],
            device_id=to_twin, device_id_type=MESH,
        )

    selected = sel_ref.shape[1]

    def selected_below(row, bound):
        found = jnp.int32(0)
        for i in range(selected):
            found += jnp.where(sel_ref[row, i] < bound, 1, 0)
        return found

    first_own = [selected_below(row, kv * kb_dev) for row in range(blocks)]

    def local_block(pair, flip, slot):
        row = 2 * pair + flip
        start = jnp.where(flip == 0, first_own[2 * pair], first_own[2 * pair + 1])
        place = jnp.minimum(start + slot, selected - 1)
        return jnp.clip(sel_ref[row, place] - kv * kb_dev, 0, kb_dev - 1)

    def fetch(block):
        return kv_v[block >> 1], block & 1

    for i in range(kv_v.shape[0]):
        load_kv(i).wait()
    for pair in range(pairs):
        for slot in range(CAP):
            tile, odd = fetch(local_block(pair, core, slot))
            left = jnp.where(odd == 1, swap_halves(tile), tile)
            tile, odd = fetch(local_block(pair, 1 - core, slot))
            right = jnp.where(odd == 0, swap_halves(tile), tile)
            ring_v[pair, slot] = jnp.where(low, left, right)
        if pair == 0:
            pl.semaphore_wait(barrier, len(partners))
        ring_copy(0, pair).start()
        twin_copy(pair).start()

    load_near.wait()
    near_copy = pltpu.make_async_remote_copy(
        src_ref=near_v.at[:, pl.ds(tok - LANES, LANES)], dst_ref=before_v,
        send_sem=near_send, recv_sem=near_recv,
        device_id=to_right, device_id_type=MESH,
    )
    near_copy.start()

    load_query.wait()
    load_uk.wait()

    def prepare(j, _):
        full = []
        for i in range(2):
            h = 2 * j + i
            absorbed = transposed_dot(uk_v[h], query_v[h, :NOPE, :]).astype(BF16)
            full.append(jnp.concatenate([absorbed, query_v[h, NOPE:, :]], axis=0))
        column = pl.ds(pl.multiple_of(j * LANES, LANES), LANES)
        for pair in range(pairs):
            a = full[0][:, pair * LANES : (pair + 1) * LANES]
            b = full[1][:, pair * LANES : (pair + 1) * LANES]
            full_v[2 * pair, :, column] = jnp.where(low, a, swap_halves(b))
            full_v[2 * pair + 1, :, column] = jnp.where(low, swap_halves(a), b)
        share = kv_total // (heads // 2)
        for row in range(blocks):
            below = selected_below(row, j * share * kb_dev)
            for i in range(share):
                holder = j * share + i
                upto = selected_below(row, (holder + 1) * kb_dev)
                count_ref[row, holder] = upto - below
                below = upto
        return 0

    lax.fori_loop(0, heads // 2, prepare, 0)

    rows = heads * BLOCK
    near_copy.wait_recv()
    token = lax.broadcasted_iota(jnp.int32, (BLOCK, rows), 1) % BLOCK
    entry = lax.broadcasted_iota(jnp.int32, (BLOCK, rows), 0)
    causal = entry <= token
    for row in range(blocks):
        tile = near_v[:, (row // 2) * LANES : (row // 2 + 1) * LANES]
        if row % 2 == 0:
            other = before_v[...] if row == 0 else near_v[:, (row // 2 - 1) * LANES : (row // 2) * LANES]
            tile = jnp.where(low, tile, other)
        scores = transposed_dot(tile, full_v[row]) * scale
        first, second = scores[:BLOCK], scores[BLOCK:]
        if row % 2 == 0:
            first = jnp.where(causal, first, NEG)
            if row == 0:
                second = jnp.where(pb > 0, second, NEG)
        else:
            second = jnp.where(causal, second, NEG)
        scores = jnp.concatenate([first, second], axis=0)
        top = jnp.max(scores, axis=0, keepdims=True)
        weights = jnp.exp2(scores - top)
        top_v[row] = top
        total_v[row] = jnp.sum(weights, axis=0, keepdims=True)
        acc_v[row] = jnp.dot(tile[:LATENT], weights.astype(BF16), preferred_element_type=F32)

    def fold(slot):
        step = slot // pairs
        pair = slot % pairs
        plus = (chip - step + chips) % chips
        minus = (chip + step) % chips
        mine = jnp.where(core == 0, 2 * plus, 2 * minus + 1)
        other = jnp.where(core == 0, 2 * minus + 1, 2 * plus)
        for half in range(2):
            row = 2 * pair + half
            mine_low = core == half
            tiles = []
            for s in range(CAP):
                own, twin = ring_v[slot, s], twin_v[slot, s]
                tiles.append(jnp.where(low == mine_low, own, twin))
            keys = jnp.concatenate(tiles, axis=1)
            low_count = jnp.where(mine_low, count_ref[row, mine], count_ref[row, other])
            high_count = jnp.where(mine_low, count_ref[row, other], count_ref[row, mine])
            scores = transposed_dot(keys, full_v[row]) * scale
            parts = []
            for s in range(CAP):
                at = 2 * s * BLOCK
                parts.append(jnp.where(low_count > s, scores[at : at + BLOCK], NEG))
                parts.append(jnp.where(high_count > s, scores[at + BLOCK : at + 2 * BLOCK], NEG))
            scores = jnp.concatenate(parts, axis=0)
            old = top_v[row]
            top = jnp.maximum(old, jnp.max(scores, axis=0, keepdims=True))
            weights = jnp.exp2(scores - top)
            factor = jnp.exp2(old - top)
            top_v[row] = top
            total_v[row] = total_v[row] * factor + jnp.sum(weights, axis=0, keepdims=True)
            acc_v[row] = acc_v[row] * factor + jnp.dot(
                keys[:LATENT], weights.astype(BF16), preferred_element_type=F32
            )

    def stage(slot, _):
        step = slot // pairs
        pair = slot % pairs
        ring_copy(step - 1, pair).wait_recv()

        @pl.when(step < chips - 1)
        def _():
            ring_copy(step, pair).start()

        twin_copy(slot).start()
        twin_copy(slot - pairs).wait_recv()
        fold(slot - pairs)
        return 0

    slots = chips * pairs
    lax.fori_loop(pairs, slots, stage, 0)
    for slot in range(slots - pairs, slots):
        twin_copy(slot).wait_recv()
        fold(slot)

    load_uv.wait()
    for row in range(blocks):
        latent = (acc_v[row] * (1.0 / total_v[row])).astype(BF16)
        for j in range(heads // 2):
            tile = latent[:, j * LANES : (j + 1) * LANES].T
            for i in range(2):
                latent_v[2 * j + i, row * BLOCK : (row + 1) * BLOCK, :] = tile[i * BLOCK : (i + 1) * BLOCK]
    for h in range(heads):
        out_ref[:, h * VDIM : (h + 1) * VDIM] = jnp.dot(
            latent_v[h], uv_v[h], preferred_element_type=F32
        ).astype(BF16)

    near_copy.wait_send()

    def drain(slot, _):
        @pl.when(slot < slots - pairs)
        def _():
            ring_copy(slot // pairs, slot % pairs).wait_send()

        twin_copy(slot).wait_send()
        return 0

    lax.fori_loop(0, slots, drain, 0)


def per_device(query, w_uk, w_uv, kv_cache, stretch_latent, selection):
    pb_total = lax.axis_size("pb")
    kv_total = lax.axis_size("kv")
    tok, heads, qwidth = query.shape
    blocks = tok // BLOCK
    pairs = blocks // 2
    chips = kv_total // 2
    scale = math.log2(math.e) / math.sqrt(qwidth)
    slots = chips * pairs
    smem = pl.BlockSpec(memory_space=pltpu.SMEM)
    anywhere = pl.BlockSpec(memory_space=pl.ANY)
    dma = pltpu.SemaphoreType.DMA
    return pl.pallas_call(
        functools.partial(kernel, pb_total, kv_total, scale),
        out_shape=jax.ShapeDtypeStruct((tok, heads * VDIM), BF16),
        in_specs=[smem] + [anywhere] * 5,
        out_specs=pl.BlockSpec(memory_space=pltpu.VMEM),
        scratch_shapes=[
            pltpu.VMEM((kv_cache.shape[0] // LANES, WIDTH, LANES), BF16),
            pltpu.VMEM((heads, qwidth, tok), BF16),
            pltpu.VMEM(w_uk.shape, BF16),
            pltpu.VMEM(w_uv.shape, BF16),
            pltpu.VMEM((WIDTH, tok), BF16),
            pltpu.VMEM((WIDTH, LANES), BF16),
            pltpu.VMEM((blocks, WIDTH, heads * BLOCK), BF16),
            pltpu.VMEM((slots, CAP, WIDTH, LANES), BF16),
            pltpu.VMEM((slots, CAP, WIDTH, LANES), BF16),
            pltpu.VMEM((blocks, LATENT, heads * BLOCK), F32),
            pltpu.VMEM((blocks, 1, heads * BLOCK), F32),
            pltpu.VMEM((blocks, 1, heads * BLOCK), F32),
            pltpu.VMEM((heads, tok, LATENT), BF16),
            pltpu.SMEM((blocks, kv_total), jnp.int32),
            dma((4,)),
            dma((kv_cache.shape[0] // LANES,)),
            dma,
            dma,
            dma((slots,)),
            dma((slots,)),
            dma((slots,)),
            dma((slots,)),
        ],
        compiler_params=pltpu.CompilerParams(
            collective_id=0, has_side_effects=True, vmem_limit_bytes=56 * 1024 * 1024
        ),
        cost_estimate=pl.CostEstimate(
            flops=2 * blocks * heads * BLOCK * 3200 * (WIDTH + LATENT),
            bytes_accessed=8 * 1024 * 1024,
            transcendentals=blocks * heads * BLOCK * 3200,
        ),
    )(
        selection,
        jnp.transpose(query, (1, 2, 0)),
        w_uk,
        w_uv,
        kv_cache.T,
        stretch_latent.T,
    )


def solution(mesh):
    placed = (
        P("pb", "kv", None),
        P("kv", None, None),
        P("kv", None, None),
        P("kv", None),
        P("pb", None),
        P("pb", None),
    )
    return jax.shard_map(
        per_device, mesh=mesh, in_specs=placed, out_specs=P("pb", "kv"), check_vma=False
    )
```

time: 188 us -> 89 us (0.47)
  Pallas kernels: 0 us -> 87 us
  waiting for transfers between devices: 76.4 us -> 0 us
  matrix products: 46.8 us -> 0 us
  local copies, waits for them, and re-layouts: 28.8 us -> 1.87 us
  other arithmetic: 17 us -> 0 us
  between operations: 13.6 us -> 0.01 us
  starting transfers between devices: 4.62 us -> 0 us
    pallas_call x0 -> x1, Pallas kernels: none -> 87 us  [per_device(): pl.pallas_call(functools.partial(kernel, pb_total, kv_total, scale), out_...]
    all_gather x1 -> x0, waiting for transfers between devices: 76.4 us -> none  [per_device(): piece = lax.all_gather(tiles, 'kv', axis=0, tiled=True)]
    dot_general x6 -> x0, matrix products: 46.8 us -> none  [the longest x2 22.2 us: online_update(): jnp.einsum('sqz,smz->sqm', query_rows, key_rows, preferred_element_type=j...]
    transpose x1 -> x0, local copies, waits for them, and re-layouts: 13.6 us -> none  [fold_tiles(): jnp.transpose(tiles_each, (1, 0, 2, 3))]
    reduce_sum x4 -> x0, other arithmetic: 12.3 us -> none  [the longest x2 12 us: online_update(): total = total * factor + jnp.sum(weights, axis=2)]
    ppermute x1 -> x0, starting transfers between devices: 4.58 us -> none  [shifted(): lax.ppermute(value, axis, [(source, source + steps) for source in range(i...]
    concatenate x1 -> x0, local copies, waits for them, and re-layouts: 3.43 us -> none  [per_device(): full = jnp.concatenate([absorbed, query[:, :, NOPE:]], axis=2)]
    reshape x3 -> x0, local copies, waits for them, and re-layouts: 3.32 us -> none  [the longest x2 2.32 us: per_device(): extended[w * BLOCK:(w + nblocks) * BLOCK].reshape(nblocks, BLOCK, width)]
  transfers between devices with their start and end apart: 2 -> 0, of which waited for: 1 -> 0; matrix products, arithmetic and copies ran while one was open for 7% -> 0% of each run, Pallas kernels for 0% -> 0%
where the time goes in v1:
time: 89 us; the launch traced here: 88.9 us
  Pallas kernels  87 us (98%)
  local copies, waits for them, and re-layouts  1.87 us (2%)
    pallas_call x1, Pallas kernels, per_device(): pl.pallas_call(functools.partial(kernel, pb_total, kv_total, scale), out_...  87 us
    unnamed x1, local copies, waits for them, and re-layouts  1.87 us

profile of v1, /device:TPU:1, one launch (start us, length us, event | category | flops | bytes accessed | tf_op | source)
XLA Modules:
  0.0 88.9 jit_solution(1617957245311636365)
XLA Ops:
  0.0 87.0 %shard_map.64 = bf16[256,1024]{1,0:T(8,128)(2,1)} custom-call(s32[4,30]{1,0:T(4,128)} %sel_ref.1, bf16[8,192,256]{2,1,0:T(8,128)(2,1)} %bitcast.4, bf16[8,128,512]{2,1,0:T(8,128)(2,1)} %uk_hbm.1, bf16[8,512,128]{2,1,0:T(8,128)(2,1)} %uv_hbm.1, bf16[576,2048]{1,0:T(8,128)(2,1)} %bitcast.3, bf16[576,256]{1,0:T(8,128)(2,1)} %bitcast.5), custom_call_target="tpu_custom_call" | custom-call | flops 14260633600 | bytes 8388608 | tf_op jit(solution)/shard_map/pallas_call | solution.py:280
  87.0 1.9 %copy.8 = bf16[256,1024]{1,0:T(8,128)(2,1)} copy(bf16[256,1024]{1,0:T(8,128)(2,1)} %shard_map.64) | data formatting | bytes 1048576
